TPU v7x, 32 devices: a whole 2x2x4 slice. The times are simulated.
32 devices in a mesh: gx: 8 (over y, x, core), gy: 4 (over z).
Axes of the slice: x: 2, y: 2, z: 4, core: 2. Of those that a mesh axis runs over, the one named last changes fastest.
Arguments:
- nest_fields: float32 [5, 80, 24, 1536], P(None, None, 'gx', 'gy'), may hold values from -6 to 6
- boundary_strip: float32 [8, 5, 80, 1536], P('gx', None, None, 'gy'), may hold values from -6 to 6
- strip_owner: int32 [4], replicated, may hold values from 0 to 7, as said below
- terrain_slope: float32 [24, 1536], P('gx', 'gy'), may hold values from -0.6 to 0.6
- column_metric: float32 [24, 1536], P('gx', 'gy'), may hold values from 0.6 to 1.6
- relax_rate: float32 [24, 1536], P('gx', 'gy'), may hold values from 0.05 to 2
- parent_state: float32 [8, 512, 320], P('gx', 'gy'), may hold values from -6 to 6
- intersection_cell: int32 [8, 4, 4, 4], P('gx', 'gy'), may hold values from 0 to 127
- intersection_row: int32 [8, 4, 4, 4], P('gx', 'gy'), may hold values from 0 to 127
- intersection_count: int32 [8, 4, 4], P('gx', 'gy'), may hold values from 1 to 4, as said below
Outputs:
- nest_out: float32 [5, 80, 24, 1536], P(None, None, 'gx', 'gy')
- parent_out: float32 [8, 512, 320], P('gx', 'gy')
Inputs may be any that keep to these rules, and one draw needn't show every extreme that they name: `strip_owner`: x index that holds the boundary rows of each y block; both 0 and 7 occur. `intersection_count`: at most 4 records go from one device to one y index; in each x group one y index receives 4 records from every device of the group.
All inputs are finite; a program needn't handle non-finite values.
Results may differ from a plain program's by a relative error of at most 0.0003.
Values sent between devices are 32-bit elements; how exact they have to be, the bound alone decides.
A program may use at most 128 MiB of HBM per device.

v0:
```python
import jax
import jax.numpy as jnp
from jax import lax
from jax.sharding import PartitionSpec as P

time_step = 0.25
sound_speed = 1.0
viscosity = 0.05
buoyancy = 0.5
wind_east = 0.6
wind_north = -0.4


def broadcast(value, axis, root):
    mine = lax.axis_index(axis) == root
    return lax.psum(jnp.where(mine, value, jnp.zeros_like(value)), axis)


def padded_2(value, sides, width):
    for axis, dim in sides:
        peers, length = (lax.axis_size(axis), value.shape[dim])
        up = [(i, (i + 1) % peers) for i in range(peers - 1)]
        down = [(j, i) for i, j in up]
        last = lax.slice_in_dim(value, length - width, length, axis=dim)
        leading = lax.slice_in_dim(value, 0, width, axis=dim)
        before = lax.ppermute(last, axis, up)
        after = lax.ppermute(leading, axis, down)
        value = jnp.concatenate([before, value, after], axis=dim)
    return value


def tendency(padded, slope, metric, relax, boundary):
    center = padded[:, :, 1:-1, 1:-1]
    east_cell = padded[:, :, 2:, 1:-1]
    west_cell = padded[:, :, :-2, 1:-1]
    north_cell = padded[:, :, 1:-1, 2:]
    south_cell = padded[:, :, 1:-1, :-2]
    vertical = jnp.pad(center, ((0, 0), (1, 1), (0, 0), (0, 0)))
    along_z = 0.5 * (vertical[:, 2:] - vertical[:, :-2]) * metric
    along_x = 0.5 * (east_cell - west_cell) - slope * along_z
    along_y = 0.5 * (north_cell - south_cell)
    spread = east_cell + west_cell + north_cell + south_cell - 4.0 * center
    common = (
        -(wind_east * along_x + wind_north * along_y)
        + viscosity * spread
        + relax * (boundary[:, :, None, :] - center)
    )
    tend_east = common[0] - sound_speed * along_x[4]
    tend_north = common[1] - sound_speed * along_y[4]
    tend_vert = common[2] - sound_speed * along_z[4] + buoyancy * center[3]
    tend_heat = common[3] - buoyancy * center[2]
    tend_press = common[4] - sound_speed * (along_x[0] + along_y[1] + along_z[2])
    return jnp.stack([tend_east, tend_north, tend_vert, tend_heat, tend_press])


def on_device(
    nest_fields,
    boundary_strip,
    strip_owner,
    terrain_slope,
    column_metric,
    relax_rate,
    parent_state,
    intersection_cell,
    intersection_row,
    intersection_count,
):
    cells_x = nest_fields.shape[2]
    cells_y = nest_fields.shape[3]
    levels = nest_fields.shape[1]
    root_index = strip_owner[lax.axis_index("gy")]
    boundary = broadcast(boundary_strip, "gx", root_index)[0]
    current = nest_fields
    for weight in (1.0 / 3.0, 0.5, 1.0):
        padded = padded_2(current, (("gx", 2), ("gy", 3)), 1)
        current = nest_fields + weight * time_step * tendency(
            padded, terrain_slope, column_metric, relax_rate, boundary
        )
    feedback_fields = jnp.stack([current[0], current[1], current[3], current[4]])
    coarse = feedback_fields.reshape(4, levels, cells_x // 3, 3, cells_y // 3, 3).mean(axis=(3, 5))
    feat_width = 4 * levels
    coarse_table = coarse.transpose(2, 3, 0, 1).reshape(-1, feat_width)
    parent_cells = parent_state.shape[1]
    capacity = intersection_cell.shape[3]
    cell_ids = intersection_cell[0, 0]
    send_counts = intersection_count[0, 0]
    active = jnp.arange(capacity)[None, :] < send_counts[:, None]
    records = coarse_table[cell_ids] * active[..., None].astype(jnp.float32)
    targets = jnp.where(active, intersection_row[0, 0], parent_cells)
    got_values, got_targets = (
        lax.all_to_all(records, "gy", split_axis=0, concat_axis=0, tiled=True),
        lax.all_to_all(targets, "gy", split_axis=0, concat_axis=0, tiled=True),
    )
    flat_values = got_values.reshape(-1, feat_width)
    flat_targets = got_targets.reshape(-1)
    onehot = (flat_targets[None, :] == jnp.arange(parent_cells)[:, None]).astype(jnp.float32)
    totals = jnp.dot(onehot, flat_values, precision=lax.Precision.HIGHEST)
    record_count = jnp.sum(onehot, axis=1)
    parent_rows = parent_state[0]
    merged = jnp.where(
        record_count[:, None] > 0, totals / jnp.maximum(record_count, 1.0)[:, None], parent_rows
    )
    return (current, merged[None])


def solution(mesh):
    placed = (
        P(None, None, "gx", "gy"),
        P("gx", None, None, "gy"),
        P(),
        P("gx", "gy"),
        P("gx", "gy"),
        P("gx", "gy"),
        P("gx", "gy", None),
        P("gx", "gy", None, None),
        P("gx", "gy", None, None),
        P("gx", "gy", None),
    )
    return jax.shard_map(
        on_device,
        mesh=mesh,
        in_specs=placed,
        out_specs=(P(None, None, "gx", "gy"), P("gx", "gy", None)),
        check_vma=False,
    )
```

profile of v0, /device:TPU:6, one launch (start us, length us, event | category | flops | bytes accessed | tf_op | source)
XLA Modules:
  0.0 192.3 jit_solution(10890411660656474874)
XLA Ops:
  7.2 2.4 %fusion.40 = (f32[5,80,1,384]{3,1,2,0:T(8,128)}, f32[5,80,1,384]{3,1,2,0:T(8,128)}) fusion(f32[5,80,3,384]{3,1,2,0:T(8,128)} %param.10), kind=kLoop, calls=%fused_computation.120 | loop fusion | bytes 2457600 | tf_op jit(solution)/shard_map/slice | solution.py:24
  9.6 2.0 %collective-permute-start.1 = (f32[5,80,1,384]{3,1,2,0:T(8,128)}, f32[5,80,1,384]{3,1,2,0:T(8,128)S(1)}, u32[]{:S(2)}, u32[]{:S(2)}) collective-permute-start(f32[5,80,1,384]{3,1,2,0:T(8,128)} %get-tuple-element.26), channel_id=1, source_target_pairs={{0,4},{4,8},{8,12},{12,16},{16,20},{20,24},{24,28},{1,5},{5,9},{9,... | collective-permute-start | bytes 1843208 | tf_op jit(solution)/shard_map/ppermute | solution.py:26
  11.7 3.6 %collective-permute-start = (f32[5,80,1,384]{3,1,2,0:T(8,128)}, f32[5,80,1,384]{3,1,2,0:T(8,128)S(1)}, u32[]{:S(2)}, u32[]{:S(2)}) collective-permute-start(f32[5,80,1,384]{3,1,2,0:T(8,128)} %get-tuple-element.27), channel_id=1, source_target_pairs={{4,0},{8,4},{12,8},{16,12},{20,16},{24,20},{28,24},{5,1},{9,5},{13... | collective-permute-start | bytes 1843208 | tf_op jit(solution)/shard_map/ppermute | solution.py:27
  15.3 0.6 dynamic_slice.3
  16.6 0.9 select_bitcast_fusion
  17.5 6.8 %collective-permute-done.1 = f32[5,80,1,384]{3,1,2,0:T(8,128)S(1)} collective-permute-done((f32[5,80,1,384]{3,1,2,0:T(8,128)}, f32[5,80,1,384]{3,1,2,0:T(8,128)S(1)}, u32[]{:S(2)}, u32[]{:S(2)}) %collective-permute-start.1) | collective-permute-done | bytes 614432 | tf_op jit(solution)/shard_map/ppermute | solution.py:26
  24.3 0.1 constant_dynamic-update-slice_fusion.1
  24.5 0.8 copy-done.13
  25.3 1.6 fusion.36
  26.9 0.4 copy-done.5
  27.3 1.8 copy.68
  29.1 1.3 collective-permute-start.2
  30.4 1.1 copy.69
  31.6 5.1 %collective-permute-start.3 = (f32[5,80,5,1]{1,2,3,0:T(8,128)}, f32[5,80,5,1]{1,2,3,0:T(8,128)}, u32[]{:S(2)}, u32[]{:S(2)}) collective-permute-start(f32[5,80,5,1]{1,2,3,0:T(8,128)} %copy.69), channel_id=1, source_target_pairs={{0,1},{1,2},{2,3},{4,5},{5,6},{6,7},{8,9},{9,10},{10,11},{12,13},{... | collective-permute-start | bytes 24008 | tf_op jit(solution)/shard_map/ppermute | solution.py:26
  36.7 0.4 copy.53
  37.1 0.7 collective-permute-done.3
  37.8 2.1 %copy.55 = f32[5,80,5,1]{3,1,2,0:T(8,128)} copy(f32[5,80,5,1]{1,2,3,0:T(8,128)} %collective-permute-done.3) | data formatting | bytes 16000 | tf_op jit(solution)/shard_map/ppermute | solution.py:26
  39.9 33.8 %all-reduce.5.cloned.1.call-done = f32[5,80,384]{2,1,0:T(8,128)} async-done(((f32[5,80,384]{2,1,0:T(8,128)}), f32[5,80,384]{2,1,0:T(8,128)}) %all-reduce.5.cloned.1.call-update) | async-done | bytes 614416 | tf_op jit(solution)/shard_map/psum | solution.py:16
  73.6 4.0 %multiply_add_fusion.5 = (f32[5,80,3,384]{3,1,2,0:T(8,128)S(1)}, f32[5,80,3,384]{3,1,2,0:T(8,128)S(1)}, f32[5,80,3,384]{3,1,2,0:T(8,128)S(1)}, f32[5,80,3,384]{3,1,2,0:T(8,128)S(1)}) fusion(f32[5,80,3,384]{3,1,2,0:T(8,128)S(1)} %copy-done, f32[5,80,1,384]{3,1,2,0:T(8,128)} %copy-done.13, f32[5,80,1,384]{3,1,2,0:T(8,128)S(1)} %collective-permute-done.1, ...), kind=kLoop, calls=%fused_computation.40 | loop fusion | flops 11980800 | bytes 14161024 | tf_op jit(solution)/shard_map/add | solution.py:44
  78.0 0.2 multiply_add_fusion.4
  78.3 1.9 collective-permute-start.4
  80.2 2.4 %collective-permute-start.5 = (f32[5,80,1,384]{3,1,2,0:T(8,128)S(1)}, f32[5,80,1,384]{3,1,2,0:T(8,128)S(1)}, u32[]{:S(2)}, u32[]{:S(2)}) collective-permute-start(f32[5,80,1,384]{3,1,2,0:T(8,128)S(1)} %get-tuple-element.24), channel_id=1, source_target_pairs={{0,4},{4,8},{8,12},{12,16},{16,20},{20,24},{24,28},{1,5},{5,9},{9,... | collective-permute-start | bytes 1843208 | tf_op jit(solution)/shard_map/ppermute | solution.py:26
  82.7 5.2 %collective-permute-done.4 = f32[5,80,1,384]{3,1,2,0:T(8,128)S(1)} collective-permute-done((f32[5,80,1,384]{3,1,2,0:T(8,128)S(1)}, f32[5,80,1,384]{3,1,2,0:T(8,128)S(1)}, u32[]{:S(2)}, u32[]{:S(2)}) %collective-permute-start.4) | collective-permute-done | bytes 614432 | tf_op jit(solution)/shard_map/ppermute | solution.py:27
  87.9 8.6 %collective-permute-done.5 = f32[5,80,1,384]{3,1,2,0:T(8,128)S(1)} collective-permute-done((f32[5,80,1,384]{3,1,2,0:T(8,128)S(1)}, f32[5,80,1,384]{3,1,2,0:T(8,128)S(1)}, u32[]{:S(2)}, u32[]{:S(2)}) %collective-permute-start.5) | collective-permute-done | bytes 614432 | tf_op jit(solution)/shard_map/ppermute | solution.py:26
  96.5 1.3 pad_maximum_fusion.23
  97.8 1.7 copy.70
  99.6 1.3 collective-permute-start.6
  100.9 1.1 copy.71
  102.0 5.1 %collective-permute-start.7 = (f32[5,80,5,1]{1,2,3,0:T(8,128)}, f32[5,80,5,1]{1,2,3,0:T(8,128)}, u32[]{:S(2)}, u32[]{:S(2)}) collective-permute-start(f32[5,80,5,1]{1,2,3,0:T(8,128)} %copy.71), channel_id=1, source_target_pairs={{0,1},{1,2},{2,3},{4,5},{5,6},{6,7},{8,9},{9,10},{10,11},{12,13},{... | collective-permute-start | bytes 24008 | tf_op jit(solution)/shard_map/ppermute | solution.py:26
  107.2 0.7 bitcast_select_fusion
  107.8 3.8 %all-to-all-start = ((s32[4,1,4]{2,1,0:T(1,128)}), s32[4,1,4]{2,1,0:T(1,128)}, u32[]{:S(2)}, u32[]{:S(2)}) async-start(s32[4,1,4]{2,1,0:T(1,128)} %bitcast.4), calls=%async_computation | async-start | bytes 4096 | tf_op jit(solution)/shard_map/all_to_all | solution.py:92
  111.6 0.4 copy.57
  112.0 2.1 %copy.59 = f32[5,80,5,1]{3,1,2,0:T(8,128)} copy(f32[5,80,5,1]{1,2,3,0:T(8,128)} %collective-permute-done.7) | data formatting | bytes 16000 | tf_op jit(solution)/shard_map/ppermute | solution.py:26
  114.1 7.3 %multiply_add_fusion.3 = (f32[5,80,3,384]{3,1,2,0:T(8,128)S(1)}, f32[5,80,3,384]{3,1,2,0:T(8,128)S(1)}, f32[5,80,3,384]{3,1,2,0:T(8,128)S(1)}) fusion(f32[5,80,3,384]{3,1,2,0:T(8,128)} %copy-done.3, f32[5,80,1,384]{3,1,2,0:T(8,128)S(1)} %collective-permute-done.4, f32[5,80,1,384]{3,1,2,0:T(8,128)} %copy-done.11, ...), kind=kLoop, calls=%fused_computation.37 | loop fusion | flops 13363200 | bytes 9245824 | tf_op jit(solution)/shard_map/add | solution.py:44
  121.5 1.2 broadcast_multiply_fusion.1
  123.0 0.2 multiply_add_fusion.2
  123.2 1.2 copy-done.1
  124.4 1.1 fusion.38
  125.6 1.9 collective-permute-start.8
  127.5 2.4 %collective-permute-start.9 = (f32[5,80,1,384]{3,1,2,0:T(8,128)}, f32[5,80,1,384]{3,1,2,0:T(8,128)S(1)}, u32[]{:S(2)}, u32[]{:S(2)}) collective-permute-start(f32[5,80,1,384]{3,1,2,0:T(8,128)} %get-tuple-element.22), channel_id=1, source_target_pairs={{0,4},{4,8},{8,12},{12,16},{16,20},{20,24},{24,28},{1,5},{5,9},{9,... | collective-permute-start | bytes 1843208 | tf_op jit(solution)/shard_map/ppermute | solution.py:26
  130.1 0.5 broadcast.149
  130.6 1.3 reduce.6
  132.2 3.3 %collective-permute-done.8 = f32[5,80,1,384]{3,1,2,0:T(8,128)S(1)} collective-permute-done((f32[5,80,1,384]{3,1,2,0:T(8,128)}, f32[5,80,1,384]{3,1,2,0:T(8,128)S(1)}, u32[]{:S(2)}, u32[]{:S(2)}) %collective-permute-start.8) | collective-permute-done | bytes 614432 | tf_op jit(solution)/shard_map/ppermute | solution.py:27
  135.4 8.3 %collective-permute-done.9 = f32[5,80,1,384]{3,1,2,0:T(8,128)S(1)} collective-permute-done((f32[5,80,1,384]{3,1,2,0:T(8,128)}, f32[5,80,1,384]{3,1,2,0:T(8,128)S(1)}, u32[]{:S(2)}, u32[]{:S(2)}) %collective-permute-start.9) | collective-permute-done | bytes 614432 | tf_op jit(solution)/shard_map/ppermute | solution.py:26
  143.8 3.2 %pad_maximum_fusion.20 = (f32[5,80,5,1]{3,1,2,0:T(8,128)}, f32[5,80,5,1]{3,1,2,0:T(8,128)}) fusion(f32[5,80,1,384]{3,1,2,0:T(8,128)S(1)} %collective-permute-done.8, f32[5,80,3,384]{3,1,2,0:T(8,128)} %copy-done.1, f32[5,80,1,384]{3,1,2,0:T(8,128)S(1)} %collective-permute-done.9), kind=kLoop, calls=%fused_computation.46 | loop fusion | flops 8000 | bytes 3088000 | tf_op jit(solution)/shard_map/concatenate | solution.py:28
  147.0 1.7 copy.72
  148.7 1.3 collective-permute-start.10
  150.0 1.7 copy.73
  151.7 5.2 %collective-permute-start.11 = (f32[5,80,5,1]{1,2,3,0:T(8,128)S(1)}, f32[5,80,5,1]{1,2,3,0:T(8,128)}, u32[]{:S(2)}, u32[]{:S(2)}) collective-permute-start(f32[5,80,5,1]{1,2,3,0:T(8,128)S(1)} %copy.73), channel_id=1, source_target_pairs={{0,1},{1,2},{2,3},{4,5},{5,6},{6,7},{8,9},{9,10},{10,11},{12,13},{... | collective-permute-start | bytes 24008 | tf_op jit(solution)/shard_map/ppermute | solution.py:26
  156.9 0.6 broadcast_compare_fusion
  157.5 0.4 copy.61
  157.9 2.1 %copy.63 = f32[5,80,5,1]{3,1,2,0:T(8,128)} copy(f32[5,80,5,1]{1,2,3,0:T(8,128)} %collective-permute-done.11) | data formatting | bytes 16000 | tf_op jit(solution)/shard_map/ppermute | solution.py:26
  160.0 7.3 %multiply_add_fusion.1 = (f32[5,80,3,384]{3,1,2,0:T(8,128)S(1)}, f32[5,80,3,384]{3,1,2,0:T(8,128)S(1)}, f32[5,80,3,384]{3,1,2,0:T(8,128)S(1)}) fusion(f32[5,80,3,384]{3,1,2,0:T(8,128)} %copy-done.1, f32[5,80,1,384]{3,1,2,0:T(8,128)S(1)} %collective-permute-done.8, f32[5,80,1,384]{3,1,2,0:T(8,128)} %copy-done.9, ...), kind=kLoop, calls=%fused_computation.34 | loop fusion | flops 13363200 | bytes 9245824 | tf_op jit(solution)/shard_map/add | solution.py:44
  167.4 1.2 broadcast_multiply_fusion
  168.9 0.2 multiply_add_fusion
  169.1 1.2 copy-done.8
  170.6 0.3 copy.65
  170.9 0.4 reduce_sum.28
  171.5 0.1 copy.67
  171.6 0.6 gather_fusion
  172.2 0.7 broadcast_multiply_fusion.3
  172.9 5.8 %all-to-all-start.1 = ((f32[4,4,320]{2,1,0:T(4,128)}), f32[4,4,320]{2,1,0:T(4,128)S(1)}, u32[]{:S(2)}, u32[]{:S(2)}) async-start(f32[4,4,320]{2,1,0:T(4,128)} %broadcast_multiply_fusion.3), calls=%async_computation.1 | async-start | bytes 49152 | tf_op jit(solution)/shard_map/all_to_all | solution.py:91
  178.7 5.6 %all-to-all-done.1 = f32[4,4,320]{2,1,0:T(4,128)S(1)} async-done(((f32[4,4,320]{2,1,0:T(4,128)}), f32[4,4,320]{2,1,0:T(4,128)S(1)}, u32[]{:S(2)}, u32[]{:S(2)}) %all-to-all-start.1) | async-done | bytes 20512 | tf_op jit(solution)/shard_map/all_to_all | solution.py:91
  184.4 1.0 fusion.7
  (91 shorter events, 2.0 us)
Async XLA Ops:
  7.2 8.1 %copy-start.23 = (s32[4]{0:T(128)S(1)}, s32[4]{0:T(128)}, u32[]{:S(2)}) copy-start(s32[4]{0:T(128)} %param.12) | copy-start | bytes 52
  7.2 66.4 %all-reduce.5.cloned.1.call-start = ((), (), s32[]{:S(2)}) async-start(), calls=%async_computation.2 | async-start | bytes 1228800 | tf_op jit(solution)/shard_map/psum | solution.py:16
  9.6 14.7 %copy-start = (f32[5,80,3,384]{3,1,2,0:T(8,128)S(1)}, f32[5,80,3,384]{3,1,2,0:T(8,128)}, u32[]{:S(2)}) copy-start(f32[5,80,3,384]{3,1,2,0:T(8,128)} %param.10) | copy-start | bytes 5529604
  9.6 14.7 %collective-permute-start.1 = (f32[5,80,1,384]{3,1,2,0:T(8,128)}, f32[5,80,1,384]{3,1,2,0:T(8,128)S(1)}, u32[]{:S(2)}, u32[]{:S(2)}) collective-permute-start(f32[5,80,1,384]{3,1,2,0:T(8,128)} %get-tuple-element.26), channel_id=1, source_target_pairs={{0,4},{4,8},{8,12},{12,16},{16,20},{20,24},{24,28},{1,5},{5,9},{9,... | collective-permute-start | bytes 1843208 | tf_op jit(solution)/shard_map/ppermute | solution.py:26
  11.7 12.8 %collective-permute-start = (f32[5,80,1,384]{3,1,2,0:T(8,128)}, f32[5,80,1,384]{3,1,2,0:T(8,128)S(1)}, u32[]{:S(2)}, u32[]{:S(2)}) collective-permute-start(f32[5,80,1,384]{3,1,2,0:T(8,128)} %get-tuple-element.27), channel_id=1, source_target_pairs={{4,0},{8,4},{12,8},{16,12},{20,16},{24,20},{28,24},{5,1},{9,5},{13... | collective-permute-start | bytes 1843208 | tf_op jit(solution)/shard_map/ppermute | solution.py:27
  24.5 0.8 copy-start.13
  25.3 2.0 %copy-start.5 = (f32[5,80,5,384]{3,1,2,0:T(8,128)}, f32[5,80,5,384]{3,1,2,0:T(8,128)S(1)}, u32[]{:S(2)}) copy-start(f32[5,80,5,384]{3,1,2,0:T(8,128)S(1)} %constant_dynamic-update-slice_fusion) | copy-start | bytes 9216004
  27.3 9.4 %copy-start.16 = (f32[3,384]{1,0:T(4,128)S(1)}, f32[3,384]{1,0:T(4,128)}, u32[]{:S(2)}) copy-start(f32[3,384]{1,0:T(4,128)} %param.14) | copy-start | bytes 13828
  27.3 46.3 %copy-start.14 = (f32[3,384]{1,0:T(4,128)S(1)}, f32[3,384]{1,0:T(4,128)}, u32[]{:S(2)}) copy-start(f32[3,384]{1,0:T(4,128)} %param.15) | copy-start | bytes 13828
  27.3 46.3 %copy-start.15 = (f32[3,384]{1,0:T(4,128)S(1)}, f32[3,384]{1,0:T(4,128)}, u32[]{:S(2)}) copy-start(f32[3,384]{1,0:T(4,128)} %param.13) | copy-start | bytes 13828
  29.1 7.6 %collective-permute-start.2 = (f32[5,80,5,1]{1,2,3,0:T(8,128)S(1)}, f32[5,80,5,1]{1,2,3,0:T(8,128)S(1)}, u32[]{:S(2)}, u32[]{:S(2)}) collective-permute-start(f32[5,80,5,1]{1,2,3,0:T(8,128)S(1)} %copy.68), channel_id=1, source_target_pairs={{1,0},{2,1},{3,2},{5,4},{6,5},{7,6},{9,8},{10,9},{11,10},{13,12},{... | collective-permute-start | bytes 24008 | tf_op jit(solution)/shard_map/ppermute | solution.py:27
  31.6 6.2 %collective-permute-start.3 = (f32[5,80,5,1]{1,2,3,0:T(8,128)}, f32[5,80,5,1]{1,2,3,0:T(8,128)}, u32[]{:S(2)}, u32[]{:S(2)}) collective-permute-start(f32[5,80,5,1]{1,2,3,0:T(8,128)} %copy.69), channel_id=1, source_target_pairs={{0,1},{1,2},{2,3},{4,5},{5,6},{6,7},{8,9},{9,10},{10,11},{12,13},{... | collective-permute-start | bytes 24008 | tf_op jit(solution)/shard_map/ppermute | solution.py:26
  78.2 19.6 %copy-start.3 = (f32[5,80,3,384]{3,1,2,0:T(8,128)}, f32[5,80,3,384]{3,1,2,0:T(8,128)S(1)}, u32[]{:S(2)}) copy-start(f32[5,80,3,384]{3,1,2,0:T(8,128)S(1)} %multiply_add_fusion.4) | copy-start | bytes 5529604
  78.3 9.6 %collective-permute-start.4 = (f32[5,80,1,384]{3,1,2,0:T(8,128)S(1)}, f32[5,80,1,384]{3,1,2,0:T(8,128)S(1)}, u32[]{:S(2)}, u32[]{:S(2)}) collective-permute-start(f32[5,80,1,384]{3,1,2,0:T(8,128)S(1)} %get-tuple-element.25), channel_id=1, source_target_pairs={{4,0},{8,4},{12,8},{16,12},{20,16},{24,20},{28,24},{5,1},{9,5},{13... | collective-permute-start | bytes 1843208 | tf_op jit(solution)/shard_map/ppermute | solution.py:27
  80.2 16.3 %collective-permute-start.5 = (f32[5,80,1,384]{3,1,2,0:T(8,128)S(1)}, f32[5,80,1,384]{3,1,2,0:T(8,128)S(1)}, u32[]{:S(2)}, u32[]{:S(2)}) collective-permute-start(f32[5,80,1,384]{3,1,2,0:T(8,128)S(1)} %get-tuple-element.24), channel_id=1, source_target_pairs={{0,4},{4,8},{8,12},{12,16},{16,20},{20,24},{24,28},{1,5},{5,9},{9,... | collective-permute-start | bytes 1843208 | tf_op jit(solution)/shard_map/ppermute | solution.py:26
  96.5 1.3 copy-start.11
  97.8 9.4 %copy-start.17 = (s32[1,1,4]{2,1,0:T(1,128)S(1)}, s32[1,1,4]{2,1,0:T(1,128)}, u32[]{:S(2)}) copy-start(s32[1,1,4]{2,1,0:T(1,128)} %param.19) | copy-start | bytes 52
  97.8 9.4 %copy-start.18 = (s32[1,1,4,4]{3,2,1,0:T(4,128)S(1)}, s32[1,1,4,4]{3,2,1,0:T(4,128)}, u32[]{:S(2)}) copy-start(s32[1,1,4,4]{3,2,1,0:T(4,128)} %param.18) | copy-start | bytes 196
  99.6 12.0 %collective-permute-start.6 = (f32[5,80,5,1]{1,2,3,0:T(8,128)S(1)}, f32[5,80,5,1]{1,2,3,0:T(8,128)S(1)}, u32[]{:S(2)}, u32[]{:S(2)}) collective-permute-start(f32[5,80,5,1]{1,2,3,0:T(8,128)S(1)} %copy.70), channel_id=1, source_target_pairs={{1,0},{2,1},{3,2},{5,4},{6,5},{7,6},{9,8},{10,9},{11,10},{13,12},{... | collective-permute-start | bytes 24008 | tf_op jit(solution)/shard_map/ppermute | solution.py:27
  102.0 10.0 %collective-permute-start.7 = (f32[5,80,5,1]{1,2,3,0:T(8,128)}, f32[5,80,5,1]{1,2,3,0:T(8,128)}, u32[]{:S(2)}, u32[]{:S(2)}) collective-permute-start(f32[5,80,5,1]{1,2,3,0:T(8,128)} %copy.71), channel_id=1, source_target_pairs={{0,1},{1,2},{2,3},{4,5},{5,6},{6,7},{8,9},{9,10},{10,11},{12,13},{... | collective-permute-start | bytes 24008 | tf_op jit(solution)/shard_map/ppermute | solution.py:26
  107.8 22.3 %all-to-all-start = ((s32[4,1,4]{2,1,0:T(1,128)}), s32[4,1,4]{2,1,0:T(1,128)}, u32[]{:S(2)}, u32[]{:S(2)}) async-start(s32[4,1,4]{2,1,0:T(1,128)} %bitcast.4), calls=%async_computation | async-start | bytes 4096 | tf_op jit(solution)/shard_map/all_to_all | solution.py:92
  114.1 7.3 %copy-start.4 = (f32[5,80,3,384]{3,1,2,0:T(8,128)S(1)}, f32[5,80,3,384]{3,1,2,0:T(8,128)}, u32[]{:S(2)}) copy-start(f32[5,80,3,384]{3,1,2,0:T(8,128)} %copy-done.3) | copy-start | bytes 5529604
  114.1 7.4 %copy-start.7 = (f32[5,80,5,1]{3,1,2,0:T(8,128)S(1)}, f32[5,80,5,1]{3,1,2,0:T(8,128)}, u32[]{:S(2)}) copy-start(f32[5,80,5,1]{3,1,2,0:T(8,128)} %copy.59) | copy-start | bytes 24004
  114.1 7.4 %copy-start.12 = (f32[5,80,1,384]{3,1,2,0:T(8,128)S(1)}, f32[5,80,1,384]{3,1,2,0:T(8,128)}, u32[]{:S(2)}) copy-start(f32[5,80,1,384]{3,1,2,0:T(8,128)} %copy-done.11) | copy-start | bytes 1843204
  123.2 1.2 copy-start.1
  124.4 5.5 %copy-start.19 = (s32[1,1,4,4]{3,2,1,0:T(4,128)S(1)}, s32[1,1,4,4]{3,2,1,0:T(4,128)}, u32[]{:S(2)}) copy-start(s32[1,1,4,4]{3,2,1,0:T(4,128)} %param.17) | copy-start | bytes 196
  125.6 9.9 %collective-permute-start.8 = (f32[5,80,1,384]{3,1,2,0:T(8,128)}, f32[5,80,1,384]{3,1,2,0:T(8,128)S(1)}, u32[]{:S(2)}, u32[]{:S(2)}) collective-permute-start(f32[5,80,1,384]{3,1,2,0:T(8,128)} %get-tuple-element.23), channel_id=1, source_target_pairs={{4,0},{8,4},{12,8},{16,12},{20,16},{24,20},{28,24},{5,1},{9,5},{13... | collective-permute-start | bytes 1843208 | tf_op jit(solution)/shard_map/ppermute | solution.py:27
  127.5 16.3 %collective-permute-start.9 = (f32[5,80,1,384]{3,1,2,0:T(8,128)}, f32[5,80,1,384]{3,1,2,0:T(8,128)S(1)}, u32[]{:S(2)}, u32[]{:S(2)}) collective-permute-start(f32[5,80,1,384]{3,1,2,0:T(8,128)} %get-tuple-element.22), channel_id=1, source_target_pairs={{0,4},{4,8},{8,12},{12,16},{16,20},{20,24},{24,28},{1,5},{5,9},{9,... | collective-permute-start | bytes 1843208 | tf_op jit(solution)/shard_map/ppermute | solution.py:26
  132.1 14.9 %copy-start.20 = (s32[16]{0:T(128)}, s32[16]{0:T(128)S(1)}, u32[]{:S(2)}) copy-start(s32[16]{0:T(128)S(1)} %eq.19) | copy-start | bytes 196
  132.2 24.7 %copy-start.24 = (f32[128]{0:T(128)}, f32[128]{0:T(128)S(1)}, u32[]{:S(2)}) copy-start(f32[128]{0:T(128)S(1)} %convert_reduce_fusion) | copy-start | bytes 1540
  143.8 3.2 %copy-start.9 = (f32[5,80,1,384]{3,1,2,0:T(8,128)}, f32[5,80,1,384]{3,1,2,0:T(8,128)S(1)}, u32[]{:S(2)}) copy-start(f32[5,80,1,384]{3,1,2,0:T(8,128)S(1)} %collective-permute-done.9) | copy-start | bytes 1843204
  148.7 8.8 %collective-permute-start.10 = (f32[5,80,5,1]{1,2,3,0:T(8,128)S(1)}, f32[5,80,5,1]{1,2,3,0:T(8,128)S(1)}, u32[]{:S(2)}, u32[]{:S(2)}) collective-permute-start(f32[5,80,5,1]{1,2,3,0:T(8,128)S(1)} %copy.72), channel_id=1, source_target_pairs={{1,0},{2,1},{3,2},{5,4},{6,5},{7,6},{9,8},{10,9},{11,10},{13,12},{... | collective-permute-start | bytes 24008 | tf_op jit(solution)/shard_map/ppermute | solution.py:27
  151.7 6.2 %collective-permute-start.11 = (f32[5,80,5,1]{1,2,3,0:T(8,128)S(1)}, f32[5,80,5,1]{1,2,3,0:T(8,128)}, u32[]{:S(2)}, u32[]{:S(2)}) collective-permute-start(f32[5,80,5,1]{1,2,3,0:T(8,128)S(1)} %copy.73), channel_id=1, source_target_pairs={{0,1},{1,2},{2,3},{4,5},{5,6},{6,7},{8,9},{9,10},{10,11},{12,13},{... | collective-permute-start | bytes 24008 | tf_op jit(solution)/shard_map/ppermute | solution.py:26
  160.0 7.4 %copy-start.2 = (f32[5,80,3,384]{3,1,2,0:T(8,128)S(1)}, f32[5,80,3,384]{3,1,2,0:T(8,128)}, u32[]{:S(2)}) copy-start(f32[5,80,3,384]{3,1,2,0:T(8,128)} %copy-done.1) | copy-start | bytes 5529604
  160.0 7.4 %copy-start.6 = (f32[5,80,5,1]{3,1,2,0:T(8,128)S(1)}, f32[5,80,5,1]{3,1,2,0:T(8,128)}, u32[]{:S(2)}) copy-start(f32[5,80,5,1]{3,1,2,0:T(8,128)} %copy.63) | copy-start | bytes 24004
  160.0 7.4 %copy-start.10 = (f32[5,80,1,384]{3,1,2,0:T(8,128)S(1)}, f32[5,80,1,384]{3,1,2,0:T(8,128)}, u32[]{:S(2)}) copy-start(f32[5,80,1,384]{3,1,2,0:T(8,128)} %copy-done.9) | copy-start | bytes 1843204
  169.1 1.2 copy-start.8
  170.5 8.2 %copy-start.25 = (f32[128]{0:T(128)S(1)}, f32[128]{0:T(128)}, u32[]{:S(2)}) copy-start(f32[128]{0:T(128)} %copy-done.24) | copy-start | bytes 1540
  170.5 13.8 %copy-start.21 = (s32[16]{0:T(128)S(1)}, s32[16]{0:T(128)}, u32[]{:S(2)}) copy-start(s32[16]{0:T(128)} %copy-done.20) | copy-start | bytes 196
  170.6 13.8 %copy-start.22 = (f32[1,128,320]{1,2,0:T(8,128)S(1)}, f32[1,128,320]{1,2,0:T(8,128)}, u32[]{:S(2)}) copy-start(f32[1,128,320]{1,2,0:T(8,128)} %param.16) | copy-start | bytes 491524
  170.6 13.8 %copy-start.26 = (pred[128]{0:T(512)(128)(4,1)S(1)}, pred[128]{0:T(512)(128)(4,1)}, u32[]{:S(2)}) copy-start(pred[128]{0:T(512)(128)(4,1)} %broadcast_compare_fusion) | copy-start | bytes 388
  172.9 11.5 %all-to-all-start.1 = ((f32[4,4,320]{2,1,0:T(4,128)}), f32[4,4,320]{2,1,0:T(4,128)S(1)}, u32[]{:S(2)}, u32[]{:S(2)}) async-start(f32[4,4,320]{2,1,0:T(4,128)} %broadcast_multiply_fusion.3), calls=%async_computation.1 | async-start | bytes 49152 | tf_op jit(solution)/shard_map/all_to_all | solution.py:91
Sparse Core Ops, SparseCore 0:
  17.6 55.9 all-reduce.4
where the time goes:
time: 193 us; the launch traced here: 192 us
  waiting for transfers between devices  72.3 us (37%)
  starting transfers between devices  43.4 us (22%)
  other arithmetic  32 us (17%)
  local copies, waits for them, and re-layouts  28.3 us (15%)
  between operations  15.2 us (8%)
    psum x1, waiting for transfers between devices, broadcast(): return lax.psum(jnp.where(mine, value, jnp.zeros_like(value)), axis)  33.8 us
    ppermute x6, waiting for transfers between devices, padded_2(): before = lax.ppermute(last, axis, up)  24.4 us
    ppermute x6, starting transfers between devices, padded_2(): before = lax.ppermute(last, axis, up)  22.4 us
    add x3, other arithmetic, tendency(): -(wind_east * along_x + wind_north * along_y) + viscosity * spread  18.6 us
    unnamed x62, local copies, waits for them, and re-layouts  13.2 us
    ppermute x6, starting transfers between devices, padded_2(): after = lax.ppermute(leading, axis, down)  11.4 us
    ppermute x6, waiting for transfers between devices, padded_2(): after = lax.ppermute(leading, axis, down)  8.5 us
    ppermute x3, local copies, waits for them, and re-layouts, padded_2(): before = lax.ppermute(last, axis, up)  6.23 us
  transfers between devices with their start and end apart: 15, of which 8 were waited for; matrix products, arithmetic and copies ran while one was open for 15% of the time, Pallas kernels for 0%

commit v1 on v0

--- a/solution.py
+++ b/solution.py
@@ -13,7 +13,7 @@
 
 def broadcast(value, axis, root):
     mine = lax.axis_index(axis) == root
-    return lax.psum(jnp.where(mine, value, jnp.zeros_like(value)), axis)
+    return lax.all_gather(jnp.where(mine, value, jnp.zeros_like(value)), axis_name=axis).sum(axis=0)
 
 
 def padded_2(value, sides, width):

time: 193 us -> 179 us (0.927)
  waiting for transfers between devices: 72.3 us -> 57.1 us
  other arithmetic: 32 us -> 35.2 us
  local copies, waits for them, and re-layouts: 28.3 us -> 26.1 us
    psum x1 -> x0, waiting for transfers between devices: 33.8 us -> none  [broadcast(): return lax.psum(jnp.where(mine, value, jnp.zeros_like(value)), axis)]
    all_gather x0 -> x1, waiting for transfers between devices: none -> 12.2 us  [broadcast(): lax.all_gather(jnp.where(mine, value, jnp.zeros_like(value)), axis_name=a...]
    ppermute x6, waiting for transfers between devices: 24.4 us -> 29.2 us  [padded_2(): before = lax.ppermute(last, axis, up)]
    reduce_sum x0 -> x1, other arithmetic: none -> 2.72 us  [broadcast(): lax.all_gather(jnp.where(mine, value, jnp.zeros_like(value)), axis_name=a...]
    slice x4, local copies, waits for them, and re-layouts: 5.19 us -> 2.8 us  [padded_2(): last = lax.slice_in_dim(value, length - width, length, axis=dim)]
    unnamed x62 -> x66, local copies, waits for them, and re-layouts: 13.2 us -> 13.3 us
  transfers between devices with their start and end apart: 15 -> 15, of which waited for: 8 -> 9; matrix products, arithmetic and copies ran while one was open for 15% -> 14% of each run, Pallas kernels for 0% -> 0%
where the time goes in v1:
time: 179 us; the launch traced here: 178 us
  waiting for transfers between devices  57.1 us (32%)
  starting transfers between devices  43.4 us (24%)
  other arithmetic  35.2 us (20%)
  local copies, waits for them, and re-layouts  26.1 us (15%)
  between operations  15.3 us (9%)
    ppermute x6, waiting for transfers between devices, padded_2(): before = lax.ppermute(last, axis, up)  29.2 us
    ppermute x6, starting transfers between devices, padded_2(): before = lax.ppermute(last, axis, up)  21.2 us
    add x3, other arithmetic, tendency(): -(wind_east * along_x + wind_north * along_y) + viscosity * spread  19.3 us
    unnamed x66, local copies, waits for them, and re-layouts  13.3 us
    ppermute x6, starting transfers between devices, padded_2(): after = lax.ppermute(leading, axis, down)  12.5 us
    all_gather x1, waiting for transfers between devices, broadcast(): lax.all_gather(jnp.where(mine, value, jnp.zeros_like(value)), axis_name=a...  12.2 us
    ppermute x6, waiting for transfers between devices, padded_2(): after = lax.ppermute(leading, axis, down)  10.1 us
    all_to_all x1, starting transfers between devices, on_device(): lax.all_to_all(records, 'gy', split_axis=0, concat_axis=0, tiled=True)  5.88 us
  transfers between devices with their start and end apart: 15, of which 9 were waited for; matrix products, arithmetic and copies ran while one was open for 14% of the time, Pallas kernels for 0%

profile of v1, /device:TPU:6, one launch (start us, length us, event | category | flops | bytes accessed | tf_op | source)
XLA Modules:
  0.0 178.0 jit_solution(4432876079178400170)
XLA Ops:
  7.2 1.4 dynamic_slice.3
  9.2 0.9 broadcast_select_fusion
  10.2 1.9 %collective-permute-start.1 = (f32[5,80,1,384]{3,1,2,0:T(8,128)S(1)}, f32[5,80,1,384]{3,1,2,0:T(8,128)S(1)}, u32[]{:S(2)}, u32[]{:S(2)}) collective-permute-start(f32[5,80,1,384]{3,1,2,0:T(8,128)S(1)} %get-tuple-element.26), channel_id=1, source_target_pairs={{0,4},{4,8},{8,12},{12,16},{16,20},{20,24},{24,28},{1,5},{5,9},{9,... | collective-permute-start | bytes 1843208 | tf_op jit(solution)/shard_map/ppermute | solution.py:26
  12.2 3.6 %collective-permute-start = (f32[5,80,1,384]{3,1,2,0:T(8,128)S(1)}, f32[5,80,1,384]{3,1,2,0:T(8,128)S(1)}, u32[]{:S(2)}, u32[]{:S(2)}) collective-permute-start(f32[5,80,1,384]{3,1,2,0:T(8,128)S(1)} %get-tuple-element.27), channel_id=1, source_target_pairs={{4,0},{8,4},{12,8},{16,12},{20,16},{24,20},{28,24},{5,1},{9,5},{13... | collective-permute-start | bytes 1843208 | tf_op jit(solution)/shard_map/ppermute | solution.py:27
  15.8 11.8 %collective-permute-done.1 = f32[5,80,1,384]{3,1,2,0:T(8,128)S(1)} collective-permute-done((f32[5,80,1,384]{3,1,2,0:T(8,128)S(1)}, f32[5,80,1,384]{3,1,2,0:T(8,128)S(1)}, u32[]{:S(2)}, u32[]{:S(2)}) %collective-permute-start.1) | collective-permute-done | bytes 614432 | tf_op jit(solution)/shard_map/ppermute | solution.py:26
  27.8 0.6 copy-done.15
  28.5 1.1 collective-permute-done
  29.6 0.9 copy-done.16
  30.5 1.5 fusion.36
  32.0 0.5 copy-done.5
  32.5 1.7 copy.67
  34.2 1.3 collective-permute-start.2
  35.5 0.5 copy.68
  36.0 4.6 %collective-permute-start.3 = (f32[5,80,5,1]{1,2,3,0:T(8,128)S(1)}, f32[5,80,5,1]{1,2,3,0:T(8,128)S(1)}, u32[]{:S(2)}, u32[]{:S(2)}) collective-permute-start(f32[5,80,5,1]{1,2,3,0:T(8,128)S(1)} %copy.68), channel_id=1, source_target_pairs={{0,1},{1,2},{2,3},{4,5},{5,6},{6,7},{8,9},{9,10},{10,11},{12,13},{... | collective-permute-start | bytes 24008 | tf_op jit(solution)/shard_map/ppermute | solution.py:26
  40.6 0.4 copy.52
  41.0 1.0 collective-permute-done.3
  42.1 1.3 copy.54
  43.4 12.2 %all-gather.3.cloned.1.call-done = f32[8,5,80,384]{3,2,1,0:T(8,128)} async-done(((f32[1,5,80,384]{3,2,1,0:T(8,128)}), f32[8,5,80,384]{3,2,1,0:T(8,128)}) %all-gather.3.cloned.1.call-update) | async-done | bytes 4915216 | tf_op jit(solution)/shard_map/all_gather | solution.py:16
  55.6 2.7 %reduce.4 = f32[5,80,384]{2,1,0:T(8,128)S(1)} reduce(f32[8,5,80,384]{3,2,1,0:T(8,128)} %all-gather.3.cloned.1.call-done, f32[]{:T(128)} %constant.18.clone.1), dimensions={0}, to_apply=%region_0.1 | reduce | flops 1075200 | bytes 5529604 | tf_op jit(solution)/shard_map/reduce_sum | solution.py:16
  58.4 4.1 %multiply_add_fusion.5 = (f32[5,80,3,384]{3,1,2,0:T(8,128)S(1)}, f32[5,80,3,384]{3,1,2,0:T(8,128)S(1)}, f32[5,80,3,384]{3,1,2,0:T(8,128)S(1)}, f32[5,80,3,384]{3,1,2,0:T(8,128)S(1)}) fusion(f32[5,80,3,384]{3,1,2,0:T(8,128)S(1)} %copy-done, f32[5,80,1,384]{3,1,2,0:T(8,128)} %copy-done.16, f32[5,80,1,384]{3,1,2,0:T(8,128)} %copy-done.15, ...), kind=kLoop, calls=%fused_computation.40 | loop fusion | flops 11980800 | bytes 14161024 | tf_op jit(solution)/shard_map/add | solution.py:44
  62.8 0.2 multiply_add_fusion.4
  63.1 3.0 %collective-permute-start.4 = (f32[5,80,1,384]{3,1,2,0:T(8,128)S(1)}, f32[5,80,1,384]{3,1,2,0:T(8,128)S(1)}, u32[]{:S(2)}, u32[]{:S(2)}) collective-permute-start(f32[5,80,1,384]{3,1,2,0:T(8,128)S(1)} %get-tuple-element.25), channel_id=1, source_target_pairs={{4,0},{8,4},{12,8},{16,12},{20,16},{24,20},{28,24},{5,1},{9,5},{13... | collective-permute-start | bytes 1843208 | tf_op jit(solution)/shard_map/ppermute | solution.py:27
  66.2 1.9 %collective-permute-start.5 = (f32[5,80,1,384]{3,1,2,0:T(8,128)S(1)}, f32[5,80,1,384]{3,1,2,0:T(8,128)S(1)}, u32[]{:S(2)}, u32[]{:S(2)}) collective-permute-start(f32[5,80,1,384]{3,1,2,0:T(8,128)S(1)} %get-tuple-element.24), channel_id=1, source_target_pairs={{0,4},{4,8},{8,12},{12,16},{16,20},{20,24},{24,28},{1,5},{5,9},{9,... | collective-permute-start | bytes 1843208 | tf_op jit(solution)/shard_map/ppermute | solution.py:26
  68.1 5.7 %collective-permute-done.4 = f32[5,80,1,384]{3,1,2,0:T(8,128)S(1)} collective-permute-done((f32[5,80,1,384]{3,1,2,0:T(8,128)S(1)}, f32[5,80,1,384]{3,1,2,0:T(8,128)S(1)}, u32[]{:S(2)}, u32[]{:S(2)}) %collective-permute-start.4) | collective-permute-done | bytes 614432 | tf_op jit(solution)/shard_map/ppermute | solution.py:27
  73.8 8.7 %collective-permute-done.5 = f32[5,80,1,384]{3,1,2,0:T(8,128)S(1)} collective-permute-done((f32[5,80,1,384]{3,1,2,0:T(8,128)S(1)}, f32[5,80,1,384]{3,1,2,0:T(8,128)S(1)}, u32[]{:S(2)}, u32[]{:S(2)}) %collective-permute-start.5) | collective-permute-done | bytes 614432 | tf_op jit(solution)/shard_map/ppermute | solution.py:26
  82.5 1.3 pad_maximum_fusion.23
  83.9 1.7 copy.69
  85.6 1.3 collective-permute-start.6
  86.9 1.1 copy.70
  88.1 5.1 %collective-permute-start.7 = (f32[5,80,5,1]{1,2,3,0:T(8,128)}, f32[5,80,5,1]{1,2,3,0:T(8,128)}, u32[]{:S(2)}, u32[]{:S(2)}) collective-permute-start(f32[5,80,5,1]{1,2,3,0:T(8,128)} %copy.70), channel_id=1, source_target_pairs={{0,1},{1,2},{2,3},{4,5},{5,6},{6,7},{8,9},{9,10},{10,11},{12,13},{... | collective-permute-start | bytes 24008 | tf_op jit(solution)/shard_map/ppermute | solution.py:26
  93.2 0.7 bitcast_select_fusion
  93.9 3.8 %all-to-all-start = ((s32[4,1,4]{2,1,0:T(1,128)}), s32[4,1,4]{2,1,0:T(1,128)}, u32[]{:S(2)}, u32[]{:S(2)}) async-start(s32[4,1,4]{2,1,0:T(1,128)} %bitcast.3), calls=%async_computation | async-start | bytes 4096 | tf_op jit(solution)/shard_map/all_to_all | solution.py:92
  97.7 0.4 copy.56
  98.1 2.1 %copy.58 = f32[5,80,5,1]{3,1,2,0:T(8,128)} copy(f32[5,80,5,1]{1,2,3,0:T(8,128)} %collective-permute-done.7) | data formatting | bytes 16000 | tf_op jit(solution)/shard_map/ppermute | solution.py:26
  100.2 7.6 %multiply_add_fusion.3 = (f32[5,80,3,384]{3,1,2,0:T(8,128)S(1)}, f32[5,80,3,384]{3,1,2,0:T(8,128)S(1)}, f32[5,80,3,384]{3,1,2,0:T(8,128)S(1)}) fusion(f32[5,80,3,384]{3,1,2,0:T(8,128)} %copy-done.3, f32[5,80,1,384]{3,1,2,0:T(8,128)} %copy-done.11, f32[5,80,1,384]{3,1,2,0:T(8,128)} %copy-done.13, f32[5,80,384]{2,1,0:T(8,128)S(1)} %reduce.4, ...), kind=kLoop, calls=%fused_computation.37 | loop fusion | flops 13363200 | bytes 9245824 | tf_op jit(solution)/shard_map/add | solution.py:44
  107.9 1.2 broadcast_multiply_fusion.1
  109.3 0.2 multiply_add_fusion.2
  109.6 1.2 copy-done.1
  110.8 1.1 fusion.38
  111.9 1.9 %collective-permute-start.8 = (f32[5,80,1,384]{3,1,2,0:T(8,128)}, f32[5,80,1,384]{3,1,2,0:T(8,128)S(1)}, u32[]{:S(2)}, u32[]{:S(2)}) collective-permute-start(f32[5,80,1,384]{3,1,2,0:T(8,128)} %get-tuple-element.23), channel_id=1, source_target_pairs={{4,0},{8,4},{12,8},{16,12},{20,16},{24,20},{28,24},{5,1},{9,5},{13... | collective-permute-start | bytes 1843208 | tf_op jit(solution)/shard_map/ppermute | solution.py:27
  113.9 2.4 %collective-permute-start.9 = (f32[5,80,1,384]{3,1,2,0:T(8,128)}, f32[5,80,1,384]{3,1,2,0:T(8,128)}, u32[]{:S(2)}, u32[]{:S(2)}) collective-permute-start(f32[5,80,1,384]{3,1,2,0:T(8,128)} %get-tuple-element.22), channel_id=1, source_target_pairs={{0,4},{4,8},{8,12},{12,16},{16,20},{20,24},{24,28},{1,5},{5,9},{9,... | collective-permute-start | bytes 1843208 | tf_op jit(solution)/shard_map/ppermute | solution.py:26
  116.5 0.5 broadcast.150
  117.0 1.3 reduce.9
  118.5 3.3 %collective-permute-done.8 = f32[5,80,1,384]{3,1,2,0:T(8,128)S(1)} collective-permute-done((f32[5,80,1,384]{3,1,2,0:T(8,128)}, f32[5,80,1,384]{3,1,2,0:T(8,128)S(1)}, u32[]{:S(2)}, u32[]{:S(2)}) %collective-permute-start.8) | collective-permute-done | bytes 614432 | tf_op jit(solution)/shard_map/ppermute | solution.py:27
  121.8 7.6 %collective-permute-done.9 = f32[5,80,1,384]{3,1,2,0:T(8,128)} collective-permute-done((f32[5,80,1,384]{3,1,2,0:T(8,128)}, f32[5,80,1,384]{3,1,2,0:T(8,128)}, u32[]{:S(2)}, u32[]{:S(2)}) %collective-permute-start.9) | collective-permute-done | bytes 614432 | tf_op jit(solution)/shard_map/ppermute | solution.py:26
  129.4 3.0 %pad_maximum_fusion.20 = (f32[5,80,5,1]{3,1,2,0:T(8,128)}, f32[5,80,5,1]{3,1,2,0:T(8,128)}) fusion(f32[5,80,1,384]{3,1,2,0:T(8,128)S(1)} %collective-permute-done.8, f32[5,80,3,384]{3,1,2,0:T(8,128)} %copy-done.1, f32[5,80,1,384]{3,1,2,0:T(8,128)} %collective-permute-done.9), kind=kLoop, calls=%fused_computation.46 | loop fusion | flops 8000 | bytes 3088000 | tf_op jit(solution)/shard_map/concatenate | solution.py:28
  132.5 1.7 copy.71
  134.2 1.3 collective-permute-start.10
  135.5 1.7 copy.72
  137.2 5.2 %collective-permute-start.11 = (f32[5,80,5,1]{1,2,3,0:T(8,128)S(1)}, f32[5,80,5,1]{1,2,3,0:T(8,128)}, u32[]{:S(2)}, u32[]{:S(2)}) collective-permute-start(f32[5,80,5,1]{1,2,3,0:T(8,128)S(1)} %copy.72), channel_id=1, source_target_pairs={{0,1},{1,2},{2,3},{4,5},{5,6},{6,7},{8,9},{9,10},{10,11},{12,13},{... | collective-permute-start | bytes 24008 | tf_op jit(solution)/shard_map/ppermute | solution.py:26
  142.4 0.5 broadcast_compare_fusion
  143.0 0.4 copy.60
  143.4 2.1 %copy.62 = f32[5,80,5,1]{3,1,2,0:T(8,128)} copy(f32[5,80,5,1]{1,2,3,0:T(8,128)} %collective-permute-done.11) | data formatting | bytes 16000 | tf_op jit(solution)/shard_map/ppermute | solution.py:26
  145.5 7.6 %multiply_add_fusion.1 = (f32[5,80,3,384]{3,1,2,0:T(8,128)S(1)}, f32[5,80,3,384]{3,1,2,0:T(8,128)S(1)}, f32[5,80,3,384]{3,1,2,0:T(8,128)S(1)}) fusion(f32[5,80,3,384]{3,1,2,0:T(8,128)} %copy-done.1, f32[5,80,1,384]{3,1,2,0:T(8,128)} %copy-done.9, f32[5,80,1,384]{3,1,2,0:T(8,128)} %collective-permute-done.9, f32[5,80,384]{2,1,0:T(8,128)S(1)} %reduce.4, ...), kind=kLoop, calls=%fused_computation.34 | loop fusion | flops 13363200 | bytes 9245824 | tf_op jit(solution)/shard_map/add | solution.py:44
  153.1 1.2 broadcast_multiply_fusion
  154.6 0.2 multiply_add_fusion
  154.9 1.2 copy-done.8
  156.3 0.3 copy.64
  156.6 0.4 reduce_sum.38
  157.3 0.6 gather_fusion
  157.9 0.7 broadcast_multiply_fusion.3
  158.6 5.9 %all-to-all-start.1 = ((f32[4,4,320]{2,1,0:T(4,128)}), f32[4,4,320]{2,1,0:T(4,128)S(1)}, u32[]{:S(2)}, u32[]{:S(2)}) async-start(f32[4,4,320]{2,1,0:T(4,128)} %broadcast_multiply_fusion.3), calls=%async_computation.1 | async-start | bytes 49152 | tf_op jit(solution)/shard_map/all_to_all | solution.py:91
  164.5 5.6 %all-to-all-done.1 = f32[4,4,320]{2,1,0:T(4,128)S(1)} async-done(((f32[4,4,320]{2,1,0:T(4,128)}), f32[4,4,320]{2,1,0:T(4,128)S(1)}, u32[]{:S(2)}, u32[]{:S(2)}) %all-to-all-start.1) | async-done | bytes 20512 | tf_op jit(solution)/shard_map/all_to_all | solution.py:91
  170.2 1.0 fusion.7
  (96 shorter events, 2.4 us)
Async XLA Ops:
  7.2 3.0 %copy-start = (f32[5,80,3,384]{3,1,2,0:T(8,128)S(1)}, f32[5,80,3,384]{3,1,2,0:T(8,128)}, u32[]{:S(2)}) copy-start(f32[5,80,3,384]{3,1,2,0:T(8,128)} %param.10) | copy-start | bytes 5529604
  7.2 48.5 %all-gather.3.cloned.1.call-start = ((), (), s32[]{:S(2)}) async-start(), calls=%async_computation.2 | async-start | bytes 5529600 | tf_op jit(solution)/shard_map/all_gather | solution.py:16
  10.2 17.4 %collective-permute-start.1 = (f32[5,80,1,384]{3,1,2,0:T(8,128)S(1)}, f32[5,80,1,384]{3,1,2,0:T(8,128)S(1)}, u32[]{:S(2)}, u32[]{:S(2)}) collective-permute-start(f32[5,80,1,384]{3,1,2,0:T(8,128)S(1)} %get-tuple-element.26), channel_id=1, source_target_pairs={{0,4},{4,8},{8,12},{12,16},{16,20},{20,24},{24,28},{1,5},{5,9},{9,... | collective-permute-start | bytes 1843208 | tf_op jit(solution)/shard_map/ppermute | solution.py:26
  12.2 17.4 %collective-permute-start = (f32[5,80,1,384]{3,1,2,0:T(8,128)S(1)}, f32[5,80,1,384]{3,1,2,0:T(8,128)S(1)}, u32[]{:S(2)}, u32[]{:S(2)}) collective-permute-start(f32[5,80,1,384]{3,1,2,0:T(8,128)S(1)} %get-tuple-element.27), channel_id=1, source_target_pairs={{4,0},{8,4},{12,8},{16,12},{20,16},{24,20},{28,24},{5,1},{9,5},{13... | collective-permute-start | bytes 1843208 | tf_op jit(solution)/shard_map/ppermute | solution.py:27
  27.6 0.8 copy-start.15
  29.5 0.9 copy-start.16
  30.5 2.0 %copy-start.5 = (f32[5,80,5,384]{3,1,2,0:T(8,128)}, f32[5,80,5,384]{3,1,2,0:T(8,128)S(1)}, u32[]{:S(2)}) copy-start(f32[5,80,5,384]{3,1,2,0:T(8,128)S(1)} %constant_dynamic-update-slice_fusion) | copy-start | bytes 9216004
  32.5 8.1 %copy-start.19 = (f32[3,384]{1,0:T(4,128)S(1)}, f32[3,384]{1,0:T(4,128)}, u32[]{:S(2)}) copy-start(f32[3,384]{1,0:T(4,128)} %param.14) | copy-start | bytes 13828
  34.2 6.4 %collective-permute-start.2 = (f32[5,80,5,1]{1,2,3,0:T(8,128)S(1)}, f32[5,80,5,1]{1,2,3,0:T(8,128)S(1)}, u32[]{:S(2)}, u32[]{:S(2)}) collective-permute-start(f32[5,80,5,1]{1,2,3,0:T(8,128)S(1)} %copy.67), channel_id=1, source_target_pairs={{1,0},{2,1},{3,2},{5,4},{6,5},{7,6},{9,8},{10,9},{11,10},{13,12},{... | collective-permute-start | bytes 24008 | tf_op jit(solution)/shard_map/ppermute | solution.py:27
  36.0 6.0 %collective-permute-start.3 = (f32[5,80,5,1]{1,2,3,0:T(8,128)S(1)}, f32[5,80,5,1]{1,2,3,0:T(8,128)S(1)}, u32[]{:S(2)}, u32[]{:S(2)}) collective-permute-start(f32[5,80,5,1]{1,2,3,0:T(8,128)S(1)} %copy.68), channel_id=1, source_target_pairs={{0,1},{1,2},{2,3},{4,5},{5,6},{6,7},{8,9},{9,10},{10,11},{12,13},{... | collective-permute-start | bytes 24008 | tf_op jit(solution)/shard_map/ppermute | solution.py:26
  43.4 14.9 %copy-start.17 = (f32[3,384]{1,0:T(4,128)S(1)}, f32[3,384]{1,0:T(4,128)}, u32[]{:S(2)}) copy-start(f32[3,384]{1,0:T(4,128)} %param.15) | copy-start | bytes 13828
  43.4 14.9 %copy-start.18 = (f32[3,384]{1,0:T(4,128)S(1)}, f32[3,384]{1,0:T(4,128)}, u32[]{:S(2)}) copy-start(f32[3,384]{1,0:T(4,128)} %param.13) | copy-start | bytes 13828
  63.0 20.8 %copy-start.3 = (f32[5,80,3,384]{3,1,2,0:T(8,128)}, f32[5,80,3,384]{3,1,2,0:T(8,128)S(1)}, u32[]{:S(2)}) copy-start(f32[5,80,3,384]{3,1,2,0:T(8,128)S(1)} %multiply_add_fusion.4) | copy-start | bytes 5529604
  63.1 10.7 %collective-permute-start.4 = (f32[5,80,1,384]{3,1,2,0:T(8,128)S(1)}, f32[5,80,1,384]{3,1,2,0:T(8,128)S(1)}, u32[]{:S(2)}, u32[]{:S(2)}) collective-permute-start(f32[5,80,1,384]{3,1,2,0:T(8,128)S(1)} %get-tuple-element.25), channel_id=1, source_target_pairs={{4,0},{8,4},{12,8},{16,12},{20,16},{24,20},{28,24},{5,1},{9,5},{13... | collective-permute-start | bytes 1843208 | tf_op jit(solution)/shard_map/ppermute | solution.py:27
  66.2 16.3 %collective-permute-start.5 = (f32[5,80,1,384]{3,1,2,0:T(8,128)S(1)}, f32[5,80,1,384]{3,1,2,0:T(8,128)S(1)}, u32[]{:S(2)}, u32[]{:S(2)}) collective-permute-start(f32[5,80,1,384]{3,1,2,0:T(8,128)S(1)} %get-tuple-element.24), channel_id=1, source_target_pairs={{0,4},{4,8},{8,12},{12,16},{16,20},{20,24},{24,28},{1,5},{5,9},{9,... | collective-permute-start | bytes 1843208 | tf_op jit(solution)/shard_map/ppermute | solution.py:26
  73.8 10.0 %copy-start.11 = (f32[5,80,1,384]{3,1,2,0:T(8,128)}, f32[5,80,1,384]{3,1,2,0:T(8,128)S(1)}, u32[]{:S(2)}) copy-start(f32[5,80,1,384]{3,1,2,0:T(8,128)S(1)} %collective-permute-done.4) | copy-start | bytes 1843204
  82.5 1.3 copy-start.13
  83.9 9.3 %copy-start.20 = (s32[1,1,4]{2,1,0:T(1,128)S(1)}, s32[1,1,4]{2,1,0:T(1,128)}, u32[]{:S(2)}) copy-start(s32[1,1,4]{2,1,0:T(1,128)} %param.19) | copy-start | bytes 52
  83.9 9.3 %copy-start.21 = (s32[1,1,4,4]{3,2,1,0:T(4,128)S(1)}, s32[1,1,4,4]{3,2,1,0:T(4,128)}, u32[]{:S(2)}) copy-start(s32[1,1,4,4]{3,2,1,0:T(4,128)} %param.18) | copy-start | bytes 196
  85.6 12.0 %collective-permute-start.6 = (f32[5,80,5,1]{1,2,3,0:T(8,128)S(1)}, f32[5,80,5,1]{1,2,3,0:T(8,128)S(1)}, u32[]{:S(2)}, u32[]{:S(2)}) collective-permute-start(f32[5,80,5,1]{1,2,3,0:T(8,128)S(1)} %copy.69), channel_id=1, source_target_pairs={{1,0},{2,1},{3,2},{5,4},{6,5},{7,6},{9,8},{10,9},{11,10},{13,12},{... | collective-permute-start | bytes 24008 | tf_op jit(solution)/shard_map/ppermute | solution.py:27
  88.1 10.0 %collective-permute-start.7 = (f32[5,80,5,1]{1,2,3,0:T(8,128)}, f32[5,80,5,1]{1,2,3,0:T(8,128)}, u32[]{:S(2)}, u32[]{:S(2)}) collective-permute-start(f32[5,80,5,1]{1,2,3,0:T(8,128)} %copy.70), channel_id=1, source_target_pairs={{0,1},{1,2},{2,3},{4,5},{5,6},{6,7},{8,9},{9,10},{10,11},{12,13},{... | collective-permute-start | bytes 24008 | tf_op jit(solution)/shard_map/ppermute | solution.py:26
  93.9 22.6 %all-to-all-start = ((s32[4,1,4]{2,1,0:T(1,128)}), s32[4,1,4]{2,1,0:T(1,128)}, u32[]{:S(2)}, u32[]{:S(2)}) async-start(s32[4,1,4]{2,1,0:T(1,128)} %bitcast.3), calls=%async_computation | async-start | bytes 4096 | tf_op jit(solution)/shard_map/all_to_all | solution.py:92
  100.1 7.7 %copy-start.4 = (f32[5,80,3,384]{3,1,2,0:T(8,128)S(1)}, f32[5,80,3,384]{3,1,2,0:T(8,128)}, u32[]{:S(2)}) copy-start(f32[5,80,3,384]{3,1,2,0:T(8,128)} %copy-done.3) | copy-start | bytes 5529604
  100.1 7.7 %copy-start.7 = (f32[5,80,5,1]{3,1,2,0:T(8,128)S(1)}, f32[5,80,5,1]{3,1,2,0:T(8,128)}, u32[]{:S(2)}) copy-start(f32[5,80,5,1]{3,1,2,0:T(8,128)} %copy.58) | copy-start | bytes 24004
  100.1 7.7 %copy-start.12 = (f32[5,80,1,384]{3,1,2,0:T(8,128)S(1)}, f32[5,80,1,384]{3,1,2,0:T(8,128)}, u32[]{:S(2)}) copy-start(f32[5,80,1,384]{3,1,2,0:T(8,128)} %copy-done.11) | copy-start | bytes 1843204
  100.2 7.7 %copy-start.14 = (f32[5,80,1,384]{3,1,2,0:T(8,128)S(1)}, f32[5,80,1,384]{3,1,2,0:T(8,128)}, u32[]{:S(2)}) copy-start(f32[5,80,1,384]{3,1,2,0:T(8,128)} %copy-done.13) | copy-start | bytes 1843204
  109.6 1.2 copy-start.1
  110.8 5.5 %copy-start.22 = (s32[1,1,4,4]{3,2,1,0:T(4,128)S(1)}, s32[1,1,4,4]{3,2,1,0:T(4,128)}, u32[]{:S(2)}) copy-start(s32[1,1,4,4]{3,2,1,0:T(4,128)} %param.17) | copy-start | bytes 196
  111.9 9.9 %collective-permute-start.8 = (f32[5,80,1,384]{3,1,2,0:T(8,128)}, f32[5,80,1,384]{3,1,2,0:T(8,128)S(1)}, u32[]{:S(2)}, u32[]{:S(2)}) collective-permute-start(f32[5,80,1,384]{3,1,2,0:T(8,128)} %get-tuple-element.23), channel_id=1, source_target_pairs={{4,0},{8,4},{12,8},{16,12},{20,16},{24,20},{28,24},{5,1},{9,5},{13... | collective-permute-start | bytes 1843208 | tf_op jit(solution)/shard_map/ppermute | solution.py:27
  113.9 15.6 %collective-permute-start.9 = (f32[5,80,1,384]{3,1,2,0:T(8,128)}, f32[5,80,1,384]{3,1,2,0:T(8,128)}, u32[]{:S(2)}, u32[]{:S(2)}) collective-permute-start(f32[5,80,1,384]{3,1,2,0:T(8,128)} %get-tuple-element.22), channel_id=1, source_target_pairs={{0,4},{4,8},{8,12},{12,16},{16,20},{20,24},{24,28},{1,5},{5,9},{9,... | collective-permute-start | bytes 1843208 | tf_op jit(solution)/shard_map/ppermute | solution.py:26
  118.4 14.0 %copy-start.23 = (s32[16]{0:T(128)}, s32[16]{0:T(128)S(1)}, u32[]{:S(2)}) copy-start(s32[16]{0:T(128)S(1)} %eq.19) | copy-start | bytes 196
  118.5 23.9 %copy-start.26 = (f32[128]{0:T(128)}, f32[128]{0:T(128)S(1)}, u32[]{:S(2)}) copy-start(f32[128]{0:T(128)S(1)} %convert_reduce_fusion) | copy-start | bytes 1540
  121.8 10.6 %copy-start.9 = (f32[5,80,1,384]{3,1,2,0:T(8,128)}, f32[5,80,1,384]{3,1,2,0:T(8,128)S(1)}, u32[]{:S(2)}) copy-start(f32[5,80,1,384]{3,1,2,0:T(8,128)S(1)} %collective-permute-done.8) | copy-start | bytes 1843204
  134.2 8.8 %collective-permute-start.10 = (f32[5,80,5,1]{1,2,3,0:T(8,128)S(1)}, f32[5,80,5,1]{1,2,3,0:T(8,128)S(1)}, u32[]{:S(2)}, u32[]{:S(2)}) collective-permute-start(f32[5,80,5,1]{1,2,3,0:T(8,128)S(1)} %copy.71), channel_id=1, source_target_pairs={{1,0},{2,1},{3,2},{5,4},{6,5},{7,6},{9,8},{10,9},{11,10},{13,12},{... | collective-permute-start | bytes 24008 | tf_op jit(solution)/shard_map/ppermute | solution.py:27
  137.2 6.1 %collective-permute-start.11 = (f32[5,80,5,1]{1,2,3,0:T(8,128)S(1)}, f32[5,80,5,1]{1,2,3,0:T(8,128)}, u32[]{:S(2)}, u32[]{:S(2)}) collective-permute-start(f32[5,80,5,1]{1,2,3,0:T(8,128)S(1)} %copy.72), channel_id=1, source_target_pairs={{0,1},{1,2},{2,3},{4,5},{5,6},{6,7},{8,9},{9,10},{10,11},{12,13},{... | collective-permute-start | bytes 24008 | tf_op jit(solution)/shard_map/ppermute | solution.py:26
  145.5 7.7 %copy-start.2 = (f32[5,80,3,384]{3,1,2,0:T(8,128)S(1)}, f32[5,80,3,384]{3,1,2,0:T(8,128)}, u32[]{:S(2)}) copy-start(f32[5,80,3,384]{3,1,2,0:T(8,128)} %copy-done.1) | copy-start | bytes 5529604
  145.5 7.7 %copy-start.6 = (f32[5,80,5,1]{3,1,2,0:T(8,128)S(1)}, f32[5,80,5,1]{3,1,2,0:T(8,128)}, u32[]{:S(2)}) copy-start(f32[5,80,5,1]{3,1,2,0:T(8,128)} %copy.62) | copy-start | bytes 24004
  145.5 7.7 %copy-start.10 = (f32[5,80,1,384]{3,1,2,0:T(8,128)S(1)}, f32[5,80,1,384]{3,1,2,0:T(8,128)}, u32[]{:S(2)}) copy-start(f32[5,80,1,384]{3,1,2,0:T(8,128)} %copy-done.9) | copy-start | bytes 1843204
  154.9 1.2 copy-start.8
  156.3 8.2 %copy-start.27 = (f32[128]{0:T(128)S(1)}, f32[128]{0:T(128)}, u32[]{:S(2)}) copy-start(f32[128]{0:T(128)} %copy-done.26) | copy-start | bytes 1540
  156.3 13.9 %copy-start.24 = (s32[16]{0:T(128)S(1)}, s32[16]{0:T(128)}, u32[]{:S(2)}) copy-start(s32[16]{0:T(128)} %copy-done.23) | copy-start | bytes 196
  156.3 13.9 %copy-start.25 = (f32[1,128,320]{1,2,0:T(8,128)S(1)}, f32[1,128,320]{1,2,0:T(8,128)}, u32[]{:S(2)}) copy-start(f32[1,128,320]{1,2,0:T(8,128)} %param.16) | copy-start | bytes 491524
  156.3 13.9 %copy-start.28 = (pred[128]{0:T(512)(128)(4,1)S(1)}, pred[128]{0:T(512)(128)(4,1)}, u32[]{:S(2)}) copy-start(pred[128]{0:T(512)(128)(4,1)} %broadcast_compare_fusion) | copy-start | bytes 388
  158.6 11.5 %all-to-all-start.1 = ((f32[4,4,320]{2,1,0:T(4,128)}), f32[4,4,320]{2,1,0:T(4,128)S(1)}, u32[]{:S(2)}, u32[]{:S(2)}) async-start(f32[4,4,320]{2,1,0:T(4,128)} %broadcast_multiply_fusion.3), calls=%async_computation.1 | async-start | bytes 49152 | tf_op jit(solution)/shard_map/all_to_all | solution.py:91
Sparse Core Ops, SparseCore 0:
  10.2 45.3 all-gather.2
